TPU v7x, 32 devices: a whole 2x2x4 slice. The times are simulated.
32 devices in a mesh: dp: 4 (over z), fsdp: 8 (over y, x, core).
Axes of the slice: x: 2, y: 2, z: 4, core: 2. Of those that a mesh axis runs over, the one named last changes fastest.
Arguments:
- tokens: bfloat16 [32768, 768], P(('dp', 'fsdp')), may hold values from -12 to 12
- lengths: int32 [32], P(('dp', 'fsdp')), may hold values from 64 to 1024, as said below
- qkv_weight: bfloat16 [768, 2304], P('fsdp'), may hold values from -0.21875 to 0.21875
- qkv_bias: bfloat16 [2304], P('fsdp'), may hold values from -1.25 to 1.25
- out_weight: bfloat16 [768, 768], P('fsdp'), may hold values from -1.75 to 1.75
- out_bias: bfloat16 [768], P('fsdp'), may hold values from -1.25 to 1.25
- fc_weight: bfloat16 [768, 3072], P('fsdp'), may hold values from -0.21875 to 0.21875
- fc_bias: bfloat16 [3072], P('fsdp'), may hold values from -1.25 to 1.25
- proj_weight: bfloat16 [3072, 768], P('fsdp'), may hold values from -0.109375 to 0.109375
- proj_bias: bfloat16 [768], P('fsdp'), may hold values from -1.25 to 1.25
- norm1_gain: bfloat16 [768], P('fsdp'), may hold values from 0.5 to 1.5
- norm1_bias: bfloat16 [768], P('fsdp'), may hold values from -1.25 to 1.25
- norm2_gain: bfloat16 [768], P('fsdp'), may hold values from 0.5 to 1.5
- norm2_bias: bfloat16 [768], P('fsdp'), may hold values from -1.25 to 1.25
- feature_map: bfloat16 [768, 128], P('fsdp'), may hold values from -0.75 to 0.75
- cotangent: bfloat16 [32768, 768], P(('dp', 'fsdp')), may hold values from -6 to 6
Outputs:
- block_out: bfloat16 [32768, 768], P(('dp', 'fsdp'))
- input_grad: bfloat16 [32768, 768], P(('dp', 'fsdp'))
- qkvw_grad: float32 [768, 2304], P('fsdp')
- qkb_grad: float32 [1536], P('fsdp')
- vb_grad: float32 [768], P('fsdp')
- outw_grad: float32 [768, 768], P('fsdp')
- outb_grad: float32 [768], P('fsdp')
- fcw_grad: float32 [768, 3072], P('fsdp')
- fcb_grad: float32 [3072], P('fsdp')
- projw_grad: float32 [3072, 768], P('fsdp')
- projb_grad: float32 [768], P('fsdp')
- gain1_grad: float32 [768], P('fsdp')
- bias1_grad: float32 [768], P('fsdp')
- gain2_grad: float32 [768], P('fsdp')
- bias2_grad: float32 [768], P('fsdp')
- fmap_grad: float32 [768, 128], P('fsdp')
Inputs may be any that keep to these rules, and one draw needn't show every extreme that they name: Sequence s has lengths[s] real tokens at the start of its 1024 rows; the rest is padding. Some sequence fills its rows and some has exactly 64.
All inputs are finite; a program needn't handle non-finite values.
Results may differ from a plain program's by a relative error of at most 0.03.
Values may be sent and summed in bfloat16 or wider, within the bound.
No kernel may reach another device: no remote copies, remote signals or barrier semaphores. Data moves between devices by JAX's collectives and lax.ppermute only.
A program may use at most 256 MiB of HBM per device.

v0:
```python
import jax
import jax.numpy as jnp
from jax import lax
from jax.sharding import PartitionSpec as P

D = 768
HEADS = 12
HD = 64
SPAN = 64
TOK_DEV = 1024


EPSILON = 1e-05
PRECISE = lax.Precision.HIGHEST


def norm_rows(values, scale_row, shift_row):
    middle = jnp.mean(values, -1, keepdims=True)
    centred = values - middle
    spread = jnp.mean(centred * centred, -1, keepdims=True)
    return centred * lax.rsqrt(spread + EPSILON) * scale_row + shift_row


def feature_pair(logits):
    return jnp.concatenate([jax.nn.softmax(logits, -1), jax.nn.softmax(-logits, -1)], -1)


def gelu_tanh(logits):
    return jax.nn.gelu(logits, approximate=True)


def earlier_sum(blocks):
    running = jnp.cumsum(blocks, 0)
    return jnp.concatenate([jnp.zeros_like(blocks[:1]), running[:-1]], 0)


def later_sum(blocks):
    running = jnp.flip(jnp.cumsum(jnp.flip(blocks, 0), 0), 0)
    return jnp.concatenate([running[1:], jnp.zeros_like(blocks[:1])], 0)


def outer_sum(left, right):
    return lax.dot_general(
        left, right, (((0,), (0,)), ((), ())), preferred_element_type=jnp.float32
    )


def back_dot(left, right):
    return lax.dot_general(
        left, right, (((1,), (1,)), ((), ())), preferred_element_type=jnp.float32
    )


def on_device(
    tokens,
    lengths,
    qkv_weight,
    qkv_bias,
    out_weight,
    out_bias,
    fc_weight,
    fc_bias,
    proj_weight,
    proj_bias,
    norm1_gain,
    norm1_bias,
    norm2_gain,
    norm2_bias,
    feature_map,
    cotangent,
):
    gathered = (
        lax.all_gather(qkv_weight, "fsdp", axis=0, tiled=True),
        lax.all_gather(qkv_bias, "fsdp", axis=0, tiled=True),
        lax.all_gather(out_weight, "fsdp", axis=0, tiled=True),
        lax.all_gather(out_bias, "fsdp", axis=0, tiled=True),
        lax.all_gather(fc_weight, "fsdp", axis=0, tiled=True),
        lax.all_gather(fc_bias, "fsdp", axis=0, tiled=True),
        lax.all_gather(proj_weight, "fsdp", axis=0, tiled=True),
        lax.all_gather(proj_bias, "fsdp", axis=0, tiled=True),
        lax.all_gather(norm1_gain, "fsdp", axis=0, tiled=True),
        lax.all_gather(norm1_bias, "fsdp", axis=0, tiled=True),
        lax.all_gather(norm2_gain, "fsdp", axis=0, tiled=True),
        lax.all_gather(norm2_bias, "fsdp", axis=0, tiled=True),
        lax.all_gather(feature_map, "fsdp", axis=0, tiled=True),
    )
    (
        wide_qkv,
        bias_qkv,
        wide_out,
        bias_out,
        wide_fc,
        bias_fc,
        wide_proj,
        bias_proj,
        gain_one,
        shift_one,
        gain_two,
        shift_two,
        wide_map,
    ) = gathered
    block_count = TOK_DEV // SPAN
    positions = jnp.arange(TOK_DEV, dtype=jnp.int32)
    live_rows = (positions < lengths[0]).astype(jnp.float32)
    live_blocks = live_rows.reshape(block_count, SPAN, 1, 1)
    lower_mask = (positions[:SPAN, None] >= positions[None, :SPAN]).astype(jnp.float32)
    inputs = tokens.astype(jnp.float32)
    hidden_one = norm_rows(
        inputs, gain_one.astype(jnp.float32), shift_one.astype(jnp.float32)
    ).astype(jnp.bfloat16)
    projected = jnp.dot(hidden_one, wide_qkv, preferred_element_type=jnp.float32) + bias_qkv.astype(
        jnp.float32
    )
    query_rows = projected[:, :D].astype(jnp.bfloat16).reshape(TOK_DEV, HEADS, HD)
    key_rows = projected[:, D : 2 * D].astype(jnp.bfloat16).reshape(TOK_DEV, HEADS, HD)
    value_rows = projected[:, 2 * D :].astype(jnp.bfloat16).reshape(TOK_DEV, HEADS, HD)
    query_map = wide_map[:, :HD].reshape(HEADS, HD, HD)
    key_map = wide_map[:, HD:].reshape(HEADS, HD, HD)
    query_logits = jnp.einsum(
        "thi,hij->thj", query_rows, query_map, preferred_element_type=jnp.float32
    )
    key_logits = jnp.einsum("thi,hij->thj", key_rows, key_map, preferred_element_type=jnp.float32)
    query_blocks = (
        feature_pair(query_logits).astype(jnp.bfloat16).reshape(block_count, SPAN, HEADS, 2 * HD)
    )
    key_blocks = (
        (feature_pair(key_logits) * live_rows[:, None, None])
        .astype(jnp.bfloat16)
        .reshape(block_count, SPAN, HEADS, 2 * HD)
    )
    value_blocks = value_rows.reshape(block_count, SPAN, HEADS, HD)
    scores = (
        jnp.einsum("nchf,ndhf->nhcd", query_blocks, key_blocks, preferred_element_type=jnp.float32)
        * lower_mask
    )
    scores_low = scores.astype(jnp.bfloat16)
    block_states = jnp.einsum(
        "ndhf,ndhe->nhfe", key_blocks, value_blocks, preferred_element_type=jnp.float32
    )
    prior_states = earlier_sum(block_states).astype(jnp.bfloat16)
    prior_totals = earlier_sum(jnp.sum(key_blocks, 1, dtype=jnp.float32))
    query_wide = query_blocks.astype(jnp.float32)
    numerator = jnp.einsum(
        "nhcd,ndhe->nche", scores_low, value_blocks, preferred_element_type=jnp.float32
    ) + jnp.einsum(
        "nchf,nhfe->nche", query_blocks, prior_states, preferred_element_type=jnp.float32
    )
    denominator = jnp.swapaxes(jnp.sum(scores, -1), 1, 2) + jnp.einsum(
        "nchf,nhf->nch", query_wide, prior_totals, precision=PRECISE
    )
    attended = (
        (numerator / denominator[..., None] * live_blocks).astype(jnp.bfloat16).reshape(TOK_DEV, D)
    )
    middle_rows = inputs + (
        jnp.dot(attended, wide_out, preferred_element_type=jnp.float32)
        + bias_out.astype(jnp.float32)
    )
    hidden_two = norm_rows(
        middle_rows, gain_two.astype(jnp.float32), shift_two.astype(jnp.float32)
    ).astype(jnp.bfloat16)
    pre_act = jnp.dot(hidden_two, wide_fc, preferred_element_type=jnp.float32) + bias_fc.astype(
        jnp.float32
    )
    activated = gelu_tanh(pre_act).astype(jnp.bfloat16)
    branch_two = jnp.dot(
        activated, wide_proj, preferred_element_type=jnp.float32
    ) + bias_proj.astype(jnp.float32)
    block_out = (middle_rows + branch_two).astype(jnp.bfloat16)
    renewed = (
        lax.all_gather(qkv_weight, "fsdp", axis=0, tiled=True),
        lax.all_gather(qkv_bias, "fsdp", axis=0, tiled=True),
        lax.all_gather(out_weight, "fsdp", axis=0, tiled=True),
        lax.all_gather(out_bias, "fsdp", axis=0, tiled=True),
        lax.all_gather(fc_weight, "fsdp", axis=0, tiled=True),
        lax.all_gather(fc_bias, "fsdp", axis=0, tiled=True),
        lax.all_gather(proj_weight, "fsdp", axis=0, tiled=True),
        lax.all_gather(proj_bias, "fsdp", axis=0, tiled=True),
        lax.all_gather(norm1_gain, "fsdp", axis=0, tiled=True),
        lax.all_gather(norm1_bias, "fsdp", axis=0, tiled=True),
        lax.all_gather(norm2_gain, "fsdp", axis=0, tiled=True),
        lax.all_gather(norm2_bias, "fsdp", axis=0, tiled=True),
        lax.all_gather(feature_map, "fsdp", axis=0, tiled=True),
    )
    (
        wide_qkv,
        bias_qkv,
        wide_out,
        bias_out,
        wide_fc,
        bias_fc,
        wide_proj,
        bias_proj,
        gain_one,
        shift_one,
        gain_two,
        shift_two,
        wide_map,
    ) = renewed
    query_map = wide_map[:, :HD].reshape(HEADS, HD, HD)
    key_map = wide_map[:, HD:].reshape(HEADS, HD, HD)
    upstream = cotangent.astype(jnp.float32)
    projw_grad = outer_sum(activated, cotangent)
    projb_grad = jnp.sum(upstream, 0)
    act_grad = back_dot(cotangent, wide_proj)
    gelu_pull = jax.vjp(gelu_tanh, pre_act)[1]
    pre_grad = gelu_pull(act_grad)[0].astype(jnp.bfloat16)
    fcw_grad = outer_sum(hidden_two, pre_grad)
    fcb_grad = jnp.sum(pre_grad, 0, dtype=jnp.float32)
    hidden_two_grad = back_dot(pre_grad, wide_fc)
    norm_pull_two = jax.vjp(
        norm_rows, middle_rows, gain_two.astype(jnp.float32), shift_two.astype(jnp.float32)
    )[1]
    middle_part, gain2_grad, bias2_grad = norm_pull_two(hidden_two_grad)
    middle_grad = upstream + middle_part
    branch_grad = middle_grad.astype(jnp.bfloat16)
    outw_grad = outer_sum(attended, branch_grad)
    outb_grad = jnp.sum(branch_grad, 0, dtype=jnp.float32)
    mixed_grad = (
        back_dot(branch_grad, wide_out).astype(jnp.bfloat16).reshape(block_count, SPAN, HEADS, HD)
    )
    masked_grad = mixed_grad.astype(jnp.float32) * live_blocks
    numer_grad = (masked_grad / denominator[..., None]).astype(jnp.bfloat16)
    denom_grad = -jnp.sum(masked_grad * numerator, -1) / (denominator * denominator)
    score_grad = (
        (
            jnp.einsum(
                "nche,ndhe->nhcd", numer_grad, value_blocks, preferred_element_type=jnp.float32
            )
            + jnp.swapaxes(denom_grad, 1, 2)[..., None]
        )
        * lower_mask
    ).astype(jnp.bfloat16)
    state_grad = jnp.einsum(
        "nchf,nche->nhfe", query_blocks, numer_grad, preferred_element_type=jnp.float32
    )
    total_grad = jnp.einsum("nchf,nch->nhf", query_wide, denom_grad, precision=PRECISE)
    block_state_grad = later_sum(state_grad).astype(jnp.bfloat16)
    key_total_grad = later_sum(total_grad)
    query_feat_grad = (
        jnp.einsum("nhcd,ndhf->nchf", score_grad, key_blocks, preferred_element_type=jnp.float32)
        + jnp.einsum(
            "nche,nhfe->nchf", numer_grad, prior_states, preferred_element_type=jnp.float32
        )
        + denom_grad[..., None] * prior_totals[:, None]
    )
    key_feat_grad = (
        jnp.einsum("nhcd,nchf->ndhf", score_grad, query_blocks, preferred_element_type=jnp.float32)
        + jnp.einsum(
            "ndhe,nhfe->ndhf", value_blocks, block_state_grad, preferred_element_type=jnp.float32
        )
        + key_total_grad[:, None]
    )
    value_grad = jnp.einsum(
        "nhcd,nche->ndhe", scores_low, numer_grad, preferred_element_type=jnp.float32
    ) + jnp.einsum(
        "ndhf,nhfe->ndhe", key_blocks, block_state_grad, preferred_element_type=jnp.float32
    )
    query_pull = jax.vjp(feature_pair, query_logits)[1]
    query_logit_grad = query_pull(query_feat_grad.reshape(TOK_DEV, HEADS, 2 * HD))[0].astype(
        jnp.bfloat16
    )
    key_pull = jax.vjp(feature_pair, key_logits)[1]
    key_logit_grad = key_pull(
        key_feat_grad.reshape(TOK_DEV, HEADS, 2 * HD) * live_rows[:, None, None]
    )[0].astype(jnp.bfloat16)
    map_query_grad = jnp.einsum(
        "thi,thj->hij", query_rows, query_logit_grad, preferred_element_type=jnp.float32
    )
    map_key_grad = jnp.einsum(
        "thi,thj->hij", key_rows, key_logit_grad, preferred_element_type=jnp.float32
    )
    fmap_grad = jnp.concatenate([map_query_grad.reshape(D, HD), map_key_grad.reshape(D, HD)], 1)
    query_grad = jnp.einsum(
        "thj,hij->thi", query_logit_grad, query_map, preferred_element_type=jnp.float32
    ).reshape(TOK_DEV, D)
    key_grad = jnp.einsum(
        "thj,hij->thi", key_logit_grad, key_map, preferred_element_type=jnp.float32
    ).reshape(TOK_DEV, D)
    project_grad = jnp.concatenate(
        [query_grad, key_grad, value_grad.reshape(TOK_DEV, D)], 1
    ).astype(jnp.bfloat16)
    qkvw_grad = outer_sum(hidden_one, project_grad)
    bias_sums = jnp.sum(project_grad, 0, dtype=jnp.float32)
    qkb_grad = bias_sums[: 2 * D]
    vb_grad = bias_sums[2 * D :]
    hidden_one_grad = back_dot(project_grad, wide_qkv)
    norm_pull_one = jax.vjp(
        norm_rows, inputs, gain_one.astype(jnp.float32), shift_one.astype(jnp.float32)
    )[1]
    input_part, gain1_grad, bias1_grad = norm_pull_one(hidden_one_grad)
    input_grad = (middle_grad + input_part).astype(jnp.bfloat16)
    shares = (
        lax.psum_scatter(qkvw_grad, "fsdp", scatter_dimension=0, tiled=True),
        lax.psum_scatter(qkb_grad, "fsdp", scatter_dimension=0, tiled=True),
        lax.psum_scatter(vb_grad, "fsdp", scatter_dimension=0, tiled=True),
        lax.psum_scatter(outw_grad, "fsdp", scatter_dimension=0, tiled=True),
        lax.psum_scatter(outb_grad, "fsdp", scatter_dimension=0, tiled=True),
        lax.psum_scatter(fcw_grad, "fsdp", scatter_dimension=0, tiled=True),
        lax.psum_scatter(fcb_grad, "fsdp", scatter_dimension=0, tiled=True),
        lax.psum_scatter(projw_grad, "fsdp", scatter_dimension=0, tiled=True),
        lax.psum_scatter(projb_grad, "fsdp", scatter_dimension=0, tiled=True),
        lax.psum_scatter(gain1_grad, "fsdp", scatter_dimension=0, tiled=True),
        lax.psum_scatter(bias1_grad, "fsdp", scatter_dimension=0, tiled=True),
        lax.psum_scatter(gain2_grad, "fsdp", scatter_dimension=0, tiled=True),
        lax.psum_scatter(bias2_grad, "fsdp", scatter_dimension=0, tiled=True),
        lax.psum_scatter(fmap_grad, "fsdp", scatter_dimension=0, tiled=True),
    )
    (
        share_qkvw,
        share_qkb,
        share_vb,
        share_outw,
        share_outb,
        share_fcw,
        share_fcb,
        share_projw,
        share_projb,
        share_gain1,
        share_bias1,
        share_gain2,
        share_bias2,
        share_fmap,
    ) = shares
    owned = (
        lax.psum(share_qkvw.astype(jnp.bfloat16), "dp").astype(jnp.float32),
        lax.psum(share_qkb.astype(jnp.bfloat16), "dp").astype(jnp.float32),
        lax.psum(share_vb.astype(jnp.bfloat16), "dp").astype(jnp.float32),
        lax.psum(share_outw.astype(jnp.bfloat16), "dp").astype(jnp.float32),
        lax.psum(share_outb.astype(jnp.bfloat16), "dp").astype(jnp.float32),
        lax.psum(share_fcw.astype(jnp.bfloat16), "dp").astype(jnp.float32),
        lax.psum(share_fcb.astype(jnp.bfloat16), "dp").astype(jnp.float32),
        lax.psum(share_projw.astype(jnp.bfloat16), "dp").astype(jnp.float32),
        lax.psum(share_projb.astype(jnp.bfloat16), "dp").astype(jnp.float32),
        lax.psum(share_gain1.astype(jnp.bfloat16), "dp").astype(jnp.float32),
        lax.psum(share_bias1.astype(jnp.bfloat16), "dp").astype(jnp.float32),
        lax.psum(share_gain2.astype(jnp.bfloat16), "dp").astype(jnp.float32),
        lax.psum(share_bias2.astype(jnp.bfloat16), "dp").astype(jnp.float32),
        lax.psum(share_fmap.astype(jnp.bfloat16), "dp").astype(jnp.float32),
    )
    (
        owned_qkvw,
        owned_qkb,
        owned_vb,
        owned_outw,
        owned_outb,
        owned_fcw,
        owned_fcb,
        owned_projw,
        owned_projb,
        owned_gain1,
        owned_bias1,
        owned_gain2,
        owned_bias2,
        owned_fmap,
    ) = owned
    return (
        block_out,
        input_grad,
        owned_qkvw,
        owned_qkb,
        owned_vb,
        owned_outw,
        owned_outb,
        owned_fcw,
        owned_fcb,
        owned_projw,
        owned_projb,
        owned_gain1,
        owned_bias1,
        owned_gain2,
        owned_bias2,
        owned_fmap,
    )


def solution(mesh):
    in_specs = (
        P(("dp", "fsdp"), None),
        P(("dp", "fsdp")),
        P("fsdp", None),
        P("fsdp"),
        P("fsdp", None),
        P("fsdp"),
        P("fsdp", None),
        P("fsdp"),
        P("fsdp", None),
        P("fsdp"),
        P("fsdp"),
        P("fsdp"),
        P("fsdp"),
        P("fsdp"),
        P("fsdp", None),
        P(("dp", "fsdp"), None),
    )
    out_specs = (
        P(("dp", "fsdp"), None),
        P(("dp", "fsdp"), None),
        P("fsdp", None),
        P("fsdp"),
        P("fsdp"),
        P("fsdp", None),
        P("fsdp"),
        P("fsdp", None),
        P("fsdp"),
        P("fsdp", None),
        P("fsdp"),
        P("fsdp"),
        P("fsdp"),
        P("fsdp"),
        P("fsdp"),
        P("fsdp", None),
    )
    return jax.shard_map(
        on_device, mesh=mesh, in_specs=in_specs, out_specs=out_specs, check_vma=False
    )
```

profile of v0, /device:TPU:0, one launch (start us, length us, event | category | flops | bytes accessed | tf_op | source)
XLA Modules:
  0.0 792.8 jit_solution(9977409187295842667)
XLA Ops:
  20.5 26.6 %all-reduce.21 = (bf16[2304]{0:T(1024)(128)(2,1)S(1)}, bf16[768]{0:T(1024)(128)(2,1)S(1)}, bf16[768]{0:T(1024)(128)(2,1)S(1)}, bf16[768]{0:T(1024)(128)(2,1)S(1)...) all-reduce(bf16[2304]{0:T(1024)(128)(2,1)S(1)} %dynamic-update-slic, ...), channel_id=1, replica_groups=mesh['dp'=4,'fsdp'=8] {'fsdp'}, use_global_device_ids=true, to_apply=%add.6 | all-reduce | flops 6912 | bytes 27648
  49.5 7.4 all-gather
  58.1 9.8 %all_gather.50 = bf16[768,128]{1,0:T(8,128)(2,1)S(1)} all-gather(bf16[96,128]{1,0:T(8,128)(2,1)} %param.30), channel_id=1, replica_groups=mesh['dp'=4,'fsdp'=8] {'fsdp'}, dimensions={0}, use_global_device_ids=true | all-gather | bytes 221184 | tf_op jit(solution)/shard_map/all_gather | solution.py:85
  72.6 6.5 add_convert_fusion
  86.0 6.1 fusion.85
  98.9 4.3 fusion.87
  103.3 5.9 reshape.316
  110.8 5.2 concatenate.36
  116.0 5.2 copy.109
  122.8 5.6 concatenate.37
  128.5 5.2 copy.110
  135.7 5.9 concatenate.39
  141.5 6.8 copy.114
  150.3 5.7 concatenate.40
  156.0 6.6 copy.115
  162.6 5.9 convert_reduce_fusion.2
  176.3 4.5 multiply_reduce_fusion
  180.8 5.0 fusion.62
  189.5 4.4 fusion.45
  193.9 9.4 %fusion.13 = (bf16[16,64,12,64]{1,3,2,0:T(8,128)(2,1)S(1)}, f32[16,12,64,64]{3,2,1,0:T(8,128)}) fusion(f32[16,64]{1,0:T(8,128)S(1)} %copy-done.85, f32[16,64,12]{1,2,0:T(8,128)S(1)} %fusion.64, f32[16,12,64,64]{3,2,1,0:T(8,128)} %fusion.45, f32[16,12,64,64]{2,3,1,0:T(8,128)} %get-tuple-element.130, f32[64,64]{0,1:T(8,128)S(1)} %copy-done.76, ...), kind=kOutput, calls=%fused_computation.23 | convolution fusion | flops 105381888 | bytes 12652544 | tf_op jit(solution)/shard_map/nhcd,ndhe->nche/dot_general | solution.py:143
  207.5 5.4 reshape.255
  220.9 11.1 %fusion.75 = f32[1024,3072]{1,0:T(8,128)} fusion(bf16[768,3072]{1,0:T(8,128)(2,1)} %all-gather.10.cloned.1.call-done, f32[1024,768]{0,1:T(8,128)} %copy-done.15, f32[768]{0:T(1024)S(1)} %convert_element_type.225, f32[768]{0:T(1024)S(1)} %convert_element_type.224, f32[1024]{0:T(1024)S(1)} %fusion.68, f32[1024]{0:T(1024)S(1)} %broadcast_multiply_fusion.1), kind=kOutput, calls=%fused_computation.150 | convolution fusion | flops 4835770368 | bytes 20461568 | tf_op jit(solution)/shard_map/dot_general | solution.py:161
  232.0 17.2 %convert_reduce_fusion = (f32[3072]{0:T(1024)}, bf16[1024,3072]{1,0:T(8,128)(2,1)S(1)}) fusion(f32[1024,3072]{1,0:T(8,128)} %fusion.75, f32[3072]{0:T(1024)S(1)} %bitcast.199, bf16[1024,768]{1,0:T(8,128)(2,1)} %param.31, bf16[3072,768]{1,0:T(8,128)(2,1)} %all-gather.12.cloned.1.call-done), kind=kOutput, calls=%fused_computation.13 | convolution fusion | flops 4904186880 | bytes 25190400 | tf_op jit(solution)/shard_map/dot_general | solution.py:49
  249.2 7.4 fusion.91
  260.5 4.5 multiply_reduce_fusion.1
  271.9 4.9 fusion.42
  276.8 6.5 reshape.306
  283.4 8.5 %copy.124 = f32[16,64,12,64]{1,3,2,0:T(8,128)} copy(f32[16,64,12,64]{3,2,1,0:T(8,128)} %reshape.306) | data formatting | bytes 6291456 | tf_op jit(solution)/shard_map/convert_element_type | solution.py:221
  291.9 8.0 %fusion.14 = (f32[16,64,12]{1,2,0:T(8,128)S(1)}, bf16[16,64,12,64]{1,3,2,0:T(8,128)(2,1)S(1)}) fusion(f32[16,64,12,64]{1,3,2,0:T(8,128)} %copy.124, f32[16,64]{1,0:T(8,128)S(1)} %copy-done.86, f32[16,12,64,64]{3,2,1,0:T(8,128)} %get-tuple-element.132, f32[16,12,64,64]{3,2,1,0:T(8,128)} %fusion.45, f32[16,64,12]{1,2,0:T(8,128)S(1)} %fusion.64), kind=kLoop, calls=%fused_computation.24 | loop fusion | flops 4706304 | bytes 11112448 | tf_op jit(solution)/shard_map/reduce_sum | solution.py:223
  311.8 4.9 multiply_convert_fusion.1
  328.4 6.9 rev.10
  344.2 6.5 fusion.101
  358.2 6.7 copy.136
  374.6 4.6 fusion.26
  384.9 10.9 %fusion.80 = (f32[1024,12,64]{2,0,1:T(8,128)}, f32[1024,12,64]{2,0,1:T(8,128)}) fusion(f32[1024,12,128]{2,0,1:T(8,128)} %bitcast.171), kind=kLoop, calls=%fused_computation.153 | loop fusion | bytes 12582912 | tf_op jit(solution)/shard_map/transpose(jvp())/split | solution.py:25
  395.8 6.3 copy.162
  404.8 6.7 copy.163
  415.4 4.8 add_convert_fusion.3
  427.6 7.1 fusion.70
  436.0 13.3 %fusion.76 = f32[3072,768]{1,0:T(8,128)} fusion(bf16[1024,768]{1,0:T(8,128)(2,1)S(1)} %copy-done.51, f32[1024,3072]{1,0:T(8,128)} %fusion.75, f32[3072]{0:T(1024)S(1)} %bitcast.200), kind=kOutput, calls=%fused_computation.151 | convolution fusion | flops 4863295488 | bytes 23605248 | tf_op jit(solution)/shard_map/dot_general | solution.py:43
  450.0 11.2 %fusion.74 = f32[768,3072]{1,0:T(8,128)} fusion(bf16[1024,3072]{1,0:T(8,128)(2,1)} %copy-done.107, f32[1024,768]{0,1:T(8,128)} %copy-done.15, f32[768]{0:T(1024)S(1)} %copy-done.75, f32[768]{0:T(1024)S(1)} %copy-done.69, f32[1024]{0:T(1024)S(1)} %copy-done.71, f32[1024]{0:T(1024)S(1)} %copy-done.66), kind=kOutput, calls=%fused_computation.149 | convolution fusion | flops 4835770368 | bytes 18888704 | tf_op jit(solution)/shard_map/dot_general | solution.py:43
  466.2 11.9 %add_convert_fusion.5 = bf16[1024,768]{0,1:T(8,128)(2,1)} fusion(f32[1024,768]{0,1:T(8,128)S(1)} %copy-done.17, bf16[3072,768]{1,0:T(8,128)(2,1)} %all-gather.12.cloned.1.call-done, f32[768]{0:T(1024)S(1)} %convert_element_type.229, f32[1024,3072]{1,0:T(8,128)} %fusion.75, f32[3072]{0:T(1024)S(1)} %bitcast.201), kind=kOutput, calls=%fused_computation.78 | convolution fusion | flops 4865654784 | bytes 22035456 | tf_op jit(solution)/shard_map/dot_general | solution.py:165
  485.4 9.6 %fusion.90 = (f32[768]{0:T(1024)S(1)}, f32[1024,768]{1,0:T(8,128)}) fusion(bf16[768,2304]{1,0:T(8,128)(2,1)} %all-gather.6.cloned.1.call-done, bf16[1024,768]{0,1:T(8,128)(2,1)} %reshape.260, bf16[1024,768]{0,1:T(8,128)(2,1)} %bitcast.184, bf16[1024,768]{0,1:T(8,128)(2,1)} %bitcast.188), kind=kOutput, calls=%fused_computation.163 | convolution fusion | flops 3638820096 | bytes 11406336 | tf_op jit(solution)/shard_map/dot_general | solution.py:49
  502.7 78.0 %reduce-scatter.12.cloned.1.call-done = f32[384,768]{1,0:T(8,128)} async-done(((f32[3072,768]{1,0:T(8,128)}), f32[384,768]{1,0:T(8,128)}) %reduce-scatter.12.cloned.1.call-update) | async-done | bytes 1179664 | tf_op jit(solution)/shard_map/reduce_scatter | solution.py:300
  582.9 77.9 %reduce-scatter.10.cloned.1.call-done = f32[96,3072]{1,0:T(8,128)} async-done(((f32[768,3072]{1,0:T(8,128)}), f32[96,3072]{1,0:T(8,128)}) %reduce-scatter.10.cloned.1.call-update) | async-done | bytes 1179664 | tf_op jit(solution)/shard_map/reduce_scatter | solution.py:298
  669.7 23.7 %all-reduce.20 = (bf16[1536]{0:T(1024)(128)(2,1)S(1)}, bf16[768]{0:T(1024)(128)(2,1)S(1)}, bf16[768]{0:T(1024)(128)(2,1)S(1)}, bf16[3072]{0:T(1024)(128)(2,1)S(1...) all-reduce(f32[1536]{0:T(1024)S(1)} %slice-done.4, ...), channel_id=3, replica_groups=mesh['dp'=4,'fsdp'=8] {'fsdp'}, use_global_device_ids=true, to_apply=%region_30.31.clone | all-reduce | flops 9984 | bytes 59904
  698.5 19.8 %all-reduce.22 = (bf16[192]{0:T(256)(128)(2,1)S(1)}, bf16[96]{0:T(256)(128)(2,1)S(1)}, bf16[96]{0:T(256)(128)(2,1)S(1)}, bf16[384]{0:T(512)(128)(2,1)S(1)}, bf16...) all-reduce(bf16[192]{0:T(256)(128)(2,1)S(1)} %dynamic-slice.35, ...), channel_id=1, replica_groups=mesh['dp'=4,'fsdp'=8] {'dp'}, use_global_device_ids=true, to_apply=%region_31.32 | all-reduce | flops 13536 | bytes 54144 | tf_op jit(solution)/shard_map/psum | solution.py:326
  723.7 55.1 %all-reduce.26.cloned.1.call-done = (bf16[96,2304]{1,0:T(8,128)(2,1)}, bf16[96,768]{1,0:T(8,128)(2,1)}, bf16[96,3072]{1,0:T(8,128)(2,1)}, bf16[384,768]{1,0:T(8,128)(2,1)}) async-done(((bf16[96,2304]{1,0:T(8,128)(2,1)}, bf16[96,768]{1,0:T(8,128)(2,1)}, bf16[96,3072]{1,0:T(8,128)(2,1)}, bf16[384,768]{1,0:T(8,128)(2,1)}), (bf16[96,2304]{1,0:T(8,128)(2,1)}, bf16[96,768]{1,0:T(8,128)(2,1)}, ...) | async-done | bytes 1769488 | tf_op jit(solution)/shard_map/psum | solution.py:325
  (394 shorter events, 191.8 us)
Async XLA Ops:
  7.2 60.9 %copy-start.49 = (bf16[1024,768]{1,0:T(8,128)(2,1)S(1)}, bf16[1024,768]{1,0:T(8,128)(2,1)}, u32[]{:S(2)}) copy-start(bf16[1024,768]{1,0:T(8,128)(2,1)} %param.16) | copy-start | bytes 4718596
  7.2 65.4 %all-gather.6.cloned.1.call-start = ((), (), s32[]{:S(2)}) async-start(), calls=%async_computation.5 | async-start | bytes 3981312 | tf_op jit(solution)/shard_map/all_gather | solution.py:73
  7.9 204.9 %all-gather.8.cloned.1.call-start = ((), (), s32[]{:S(2)}) async-start(), calls=%async_computation.6 | async-start | bytes 1327104 | tf_op jit(solution)/shard_map/all_gather | solution.py:75
  8.7 212.2 %all-gather.10.cloned.1.call-start = ((), (), s32[]{:S(2)}) async-start(), calls=%async_computation.7 | async-start | bytes 5308416 | tf_op jit(solution)/shard_map/all_gather | solution.py:77
  9.4 222.6 %all-gather.12.cloned.1.call-start = ((), (), s32[]{:S(2)}) async-start(), calls=%async_computation.8 | async-start | bytes 5308416 | tf_op jit(solution)/shard_map/all_gather | solution.py:79
  10.0 488.7 %reduce-scatter.8.cloned.1.call-start = ((), (), s32[]{:S(2)}) async-start(), calls=%async_computation.10 | async-start | bytes 2654208 | tf_op jit(solution)/shard_map/reduce_scatter | solution.py:296
  47.1 25.6 %copy-start.87 = (f32[768]{0:T(1024)}, f32[768]{0:T(1024)S(1)}, u32[]{:S(2)}) copy-start(f32[768]{0:T(1024)S(1)} %convert_element_type.213) | copy-start | bytes 9220
  47.1 218.0 %copy-start.68 = (f32[768]{0:T(1024)}, f32[768]{0:T(1024)S(1)}, u32[]{:S(2)}) copy-start(f32[768]{0:T(1024)S(1)} %convert_element_type.224) | copy-start | bytes 9220
  47.7 173.2 %copy-start.74 = (f32[768]{0:T(1024)}, f32[768]{0:T(1024)S(1)}, u32[]{:S(2)}) copy-start(f32[768]{0:T(1024)S(1)} %convert_element_type.225) | copy-start | bytes 9220
  68.0 18.0 %copy-start.45 = (bf16[768,64]{1,0:T(8,128)(2,1)}, bf16[768,64]{1,0:T(8,128)(2,1)S(1)}, u32[]{:S(2)}) copy-start(bf16[768,64]{1,0:T(8,128)(2,1)S(1)} %get-tuple-element.116) | copy-start | bytes 294916
  68.1 30.9 %copy-start.47 = (bf16[768,64]{1,0:T(8,128)(2,1)}, bf16[768,64]{1,0:T(8,128)(2,1)S(1)}, u32[]{:S(2)}) copy-start(bf16[768,64]{1,0:T(8,128)(2,1)S(1)} %get-tuple-element.115) | copy-start | bytes 294916
  69.3 9.8 %copy-start.82 = (f32[1024]{0:T(1024)}, f32[1024]{0:T(1024)S(1)}, u32[]{:S(2)}) copy-start(f32[1024]{0:T(1024)S(1)} %broadcast_multiply_fusion.2) | copy-start | bytes 12292
  86.0 23.2 %copy-start.10 = (f32[1024,12,64]{0,2,1:T(8,128)}, f32[1024,12,64]{0,2,1:T(8,128)S(1)}, u32[]{:S(2)}) copy-start(f32[1024,12,64]{0,2,1:T(8,128)S(1)} %get-tuple-element.124) | copy-start | bytes 9437188
  98.9 34.7 %copy-start.58 = (f32[1024,12]{0,1:T(8,128)}, f32[1024,12]{0,1:T(8,128)S(1)}, u32[]{:S(2)}) copy-start(f32[1024,12]{0,1:T(8,128)S(1)} %get-tuple-element.127) | copy-start | bytes 147460
  103.3 45.0 %copy-start.61 = (f32[1024,12]{0,1:T(8,128)}, f32[1024,12]{0,1:T(8,128)S(1)}, u32[]{:S(2)}) copy-start(f32[1024,12]{0,1:T(8,128)S(1)} %get-tuple-element.125) | copy-start | bytes 147460
  103.3 5.9 copy-start.54
  141.5 6.8 copy-start.21
  156.0 6.6 copy-start.84
  162.6 7.6 copy-start.38
  162.6 7.6 copy-start.39
  168.5 7.8 copy-start
  172.0 17.5 %copy-start.2 = (bf16[16,64,12,128]{3,1,2,0:T(8,128)(2,1)}, bf16[16,64,12,128]{3,1,2,0:T(8,128)(2,1)S(1)}, u32[]{:S(2)}) copy-start(bf16[16,64,12,128]{3,1,2,0:T(8,128)(2,1)S(1)} %pad_maximum_fusion.1) | copy-start | bytes 9437188
  207.5 5.4 copy-start.105
  216.8 48.3 %copy-start.65 = (f32[1024]{0:T(1024)}, f32[1024]{0:T(1024)S(1)}, u32[]{:S(2)}) copy-start(f32[1024]{0:T(1024)S(1)} %broadcast_multiply_fusion.1) | copy-start | bytes 12292
  218.9 46.2 %copy-start.70 = (f32[1024]{0:T(1024)}, f32[1024]{0:T(1024)S(1)}, u32[]{:S(2)}) copy-start(f32[1024]{0:T(1024)S(1)} %fusion.68) | copy-start | bytes 12292
  220.9 11.1 %copy-start.100 = (f32[8,1,384]{2,1,0:T(1,128)S(1)}, f32[8,1,384]{2,1,0:T(1,128)}, u32[]{:S(2)}) copy-start(f32[8,1,384]{2,1,0:T(1,128)} %convert_element_type.275) | copy-start | bytes 36868
  232.0 17.2 %copy-start.44 = (bf16[768,3072]{1,0:T(8,128)(2,1)S(1)}, bf16[768,3072]{1,0:T(8,128)(2,1)}, u32[]{:S(2)}) copy-start(bf16[768,3072]{1,0:T(8,128)(2,1)} %all-gather.10.cloned.1.call-done) | copy-start | bytes 14155780
  249.2 7.4 copy-start.107
  283.4 8.5 %copy-start.86 = (f32[16,64]{1,0:T(8,128)S(1)}, f32[16,64]{1,0:T(8,128)}, u32[]{:S(2)}) copy-start(f32[16,64]{1,0:T(8,128)} %fusion.65) | copy-start | bytes 12292
  291.9 8.0 %copy-start.73 = (f32[16,12,1,64]{3,2,1,0:T(1,128)S(1)}, f32[16,12,1,64]{3,2,1,0:T(1,128)}, u32[]{:S(2)}) copy-start(f32[16,12,1,64]{3,2,1,0:T(1,128)} %copy-done.72) | copy-start | bytes 147460
  308.2 192.5 %reduce-scatter.6.cloned.1.call-start = ((), (), s32[]{:S(2)}) async-start(), calls=%async_computation.9 | async-start | bytes 7962624 | tf_op jit(solution)/shard_map/reduce_scatter | solution.py:293
  311.7 9.1 %slice-start.2 = ((s8[6291456]{0:T(1024)(128)(4,1)}), s8[4194304]{0:T(1024)(128)(4,1)S(1)}, s32[]{:S(2)}) async-start(s8[6291456]{0:T(1024)(128)(4,1)} %bitcast.180), calls=%async_computation.17 | async-start | bytes 8388608
  344.2 6.5 copy-start.31
  358.2 6.8 copy-start.98
  365.0 8.1 %slice-start = ((s8[6291456]{0:T(1024)(128)(4,1)}), s8[4194304]{0:T(1024)(128)(4,1)S(1)}, s32[]{:S(2)}) async-start(s8[6291456]{0:T(1024)(128)(4,1)} %bitcast.178), calls=%async_computation.15 | async-start | bytes 8388608
  395.8 6.3 copy-start.13
  395.8 6.3 copy-start.79
  404.8 6.7 copy-start.11
  404.8 6.7 copy-start.78
  415.3 5.4 copy-start.25
  415.3 5.5 copy-start.26
  434.6 146.1 %reduce-scatter.12.cloned.1.call-start = ((), (), s32[]{:S(2)}) async-start(), calls=%async_computation.12 | async-start | bytes 10616832 | tf_op jit(solution)/shard_map/reduce_scatter | solution.py:300
  449.3 211.4 %reduce-scatter.10.cloned.1.call-start = ((), (), s32[]{:S(2)}) async-start(), calls=%async_computation.11 | async-start | bytes 10616832 | tf_op jit(solution)/shard_map/reduce_scatter | solution.py:298
  461.3 236.4 %reduce-scatter.14.cloned.1.call-start = ((), (), s32[]{:S(2)}) async-start(), calls=%async_computation.13 | async-start | bytes 442368 | tf_op jit(solution)/shard_map/reduce_scatter | solution.py:306
  465.8 12.3 %copy-start.89 = (f32[2304]{0:T(1024)}, f32[2304]{0:T(1024)S(1)}, u32[]{:S(2)}) copy-start(f32[2304]{0:T(1024)S(1)} %convert_reduce_fusion.1) | copy-start | bytes 27652
  478.1 5.4 copy-start.32
  485.2 293.7 %all-reduce.26.cloned.1.call-start = ((), (), s32[]{:S(2)}) async-start(), calls=%async_computation.14 | async-start | bytes 3538944 | tf_op jit(solution)/shard_map/psum | solution.py:325
  778.8 5.9 copy-start.64
  (75 other events, 220.4 us)
Sparse Core Ops, SparseCore 0:
  9.9 36.9 all-gather.5
  48.8 24.0 all-gather.7
  74.8 38.9 all-gather.9
  115.5 38.8 all-gather.11
  308.3 42.8 reduce-scatter.7
  434.8 65.9 reduce-scatter.5
  504.3 76.4 reduce-scatter.11
  584.3 76.4 reduce-scatter.9
  663.8 33.8 reduce-scatter.13
  701.3 77.4 all-reduce.25
where the time goes:
time: 798 us; the launch traced here: 793 us
  waiting for transfers between devices  216 us (27%)
  matrix products  194 us (24%)
  local copies, waits for them, and re-layouts  180 us (23%)
  other arithmetic  94.8 us (12%)
  blocking collectives  87.3 us (11%)
  between operations  19.6 us (2%)
    reduce_scatter x1, waiting for transfers between devices, on_device(): lax.psum_scatter(projw_grad, 'fsdp', scatter_dimension=0, tiled=True)  78 us
    reduce_scatter x1, waiting for transfers between devices, on_device(): lax.psum_scatter(fcw_grad, 'fsdp', scatter_dimension=0, tiled=True)  77.9 us
    psum x1, waiting for transfers between devices, on_device(): lax.psum(share_qkvw.astype(jnp.bfloat16), 'dp').astype(jnp.float32)  55.1 us
    unnamed x2, blocking collectives  50.3 us
    unnamed x255, local copies, waits for them, and re-layouts  46.3 us
    concatenate x8, local copies, waits for them, and re-layouts, feature_pair(): jnp.concatenate([jax.nn.softmax(logits, -1), jax.nn.softmax(-logits, -1)]...  46.2 us
    dot_general x4, matrix products, back_dot(): lax.dot_general(left, right, (((1,), (1,)), ((), ())), preferred_element_...  39.1 us
    dot_general x4, matrix products, outer_sum(): lax.dot_general(left, right, (((0,), (0,)), ((), ())), preferred_element_...  34.6 us
  transfers between devices with their start and end apart: 10, of which 5 were waited for; matrix products, arithmetic and copies ran while one was open for 47% of the time, Pallas kernels for 0%

commit v1 on v0

v1 whole, which is shorter than its diff:
```python
import functools

import jax
import jax.numpy as jnp
from jax import lax
from jax.experimental import pallas as pl
from jax.experimental.pallas import tpu as pltpu
from jax.sharding import PartitionSpec as P

D = 768
HEADS = 12
HD = 64
PAIRS = HEADS // 2
FF = 3072
ROWS = 256
CHUNK = 128
EPSILON = 1e-05
SAFE = 60.0
VMEM = 56 * 1024 * 1024
F32 = jnp.float32
BF16 = jnp.bfloat16


def nn(left, right):
    return lax.dot_general(left, right, (((1,), (0,)), ((), ())), preferred_element_type=F32)


def nt(left, right):
    return lax.dot_general(left, right, (((1,), (1,)), ((), ())), preferred_element_type=F32)


def tn(left, right):
    return lax.dot_general(left, right, (((0,), (0,)), ((), ())), preferred_element_type=F32)


def params(*semantics):
    return pltpu.CompilerParams(vmem_limit_bytes=VMEM, dimension_semantics=semantics or None)


def lanes(shape):
    return lax.broadcasted_iota(jnp.int32, shape, 1)


def inverse(values):
    first = pl.reciprocal(values, approx=True)
    return first * (2.0 - values * first)


def normalized(values):
    middle = jnp.mean(values, -1, keepdims=True)
    centred = values - middle
    spread = jnp.mean(centred * centred, -1, keepdims=True)
    scale = lax.rsqrt(spread + EPSILON)
    return centred * scale, scale


def norm_back(grad, gain, unit, scale):
    scaled = grad * gain
    first = jnp.mean(scaled, -1, keepdims=True)
    second = jnp.mean(scaled * unit, -1, keepdims=True)
    return (scaled - first - unit * second) * scale


def swap_halves(values):
    return pltpu.roll(values, 64, 1)


def block_ones(size):
    row = lax.broadcasted_iota(jnp.int32, (size, size), 0) // HD
    col = lax.broadcasted_iota(jnp.int32, (size, size), 1) // HD
    return jnp.where(row == col, 1.0, 0.0).astype(BF16)


def build_maps(map_ref, fq, fk):
    fq[...] = jnp.zeros_like(fq)
    fk[...] = jnp.zeros_like(fk)
    low = lanes((HD, 2 * HD)) < HD
    for head in range(HEADS):
        block = map_ref[head * HD : (head + 1) * HD, :].astype(F32)
        turned = swap_halves(block)
        row, col = (head % 2) * HD, (head % 2) * 2 * HD
        fq[head // 2, row : row + HD, col : col + 2 * HD] = jnp.where(low, block, -turned).astype(BF16)
        fk[head // 2, row : row + HD, col : col + 2 * HD] = jnp.where(low, turned, -block).astype(BF16)


def qkv_kernel(
    len_ref, tok_ref, w_ref, bias_ref, gain_ref, shift_ref, map_ref,
    h_ref, q_ref, k_ref, v_ref, pq_ref, pk_ref, fq, fk, ones, u,
):
    step = pl.program_id(0)

    @pl.when(step == 0)
    def _():
        build_maps(map_ref, fq, fk)
        ones[...] = block_ones(4 * HD)

    unit, _ = normalized(tok_ref[...].astype(F32))
    h = (unit * gain_ref[...] + shift_ref[...]).astype(BF16)
    h_ref[...] = h
    for part, (out, maps) in enumerate(((q_ref, fq), (k_ref, fk), (v_ref, None))):
        cols = slice(part * D, (part + 1) * D)
        rows = (nn(h, w_ref[:, cols]) + bias_ref[:, cols]).astype(BF16)
        out[...] = rows
        if maps is None:
            continue
        for pair in range(PAIRS):
            u[:, part * 2 * D + pair * 256 : part * 2 * D + (pair + 1) * 256] = nn(
                rows[:, pair * 128 : (pair + 1) * 128], maps[pair]
            )

    @pl.when(jnp.max(u[...]) > SAFE)
    def _():
        for group in range(4 * HEADS):
            cols = slice(group * HD, (group + 1) * HD)
            piece = u[:, cols]
            u[:, cols] = piece - jnp.max(piece, -1, keepdims=True)

    rows = step * ROWS + lax.broadcasted_iota(jnp.int32, (ROWS, 1), 0)
    live = (rows < len_ref[0]).astype(F32)
    for part, out in enumerate((pq_ref, pk_ref)):
        for pair in range(PAIRS):
            cols = slice(pair * 256, (pair + 1) * 256)
            e = jnp.exp(u[:, part * 2 * D + pair * 256 : part * 2 * D + (pair + 1) * 256])
            total = nn(e.astype(BF16), ones[...])
            share = e * inverse(total)
            if part == 1:
                share = share * live
            out[:, cols] = share.astype(BF16)


def whole(shape, single=True):
    zeros = (0,) * len(shape)
    if single:
        return pl.BlockSpec(shape, lambda *_: zeros, pipeline_mode=pl.Buffered(1))
    return pl.BlockSpec(shape, lambda *_: zeros)


def rows_of(count, width):
    return pl.BlockSpec((count, width), lambda i, *_: (i, 0))


SMEM = pl.BlockSpec(memory_space=pltpu.SMEM)


def cost(flops, size, trans=0):
    return pl.CostEstimate(flops=int(flops), bytes_accessed=int(size), transcendentals=int(trans))


def project(lengths, tokens, w, bias, gain, shift, fmap):
    count = tokens.shape[0]
    shape = lambda width: jax.ShapeDtypeStruct((count, width), BF16)
    return pl.pallas_call(
        qkv_kernel,
        name="project",
        grid=(count // ROWS,),
        in_specs=[
            SMEM, rows_of(ROWS, D), whole((D, 3 * D)), whole((1, 3 * D)), whole((1, D)), whole((1, D)), whole((D, 2 * HD)),
        ],
        out_specs=[rows_of(ROWS, D)] * 4 + [rows_of(ROWS, 2 * D)] * 2,
        out_shape=[shape(D)] * 4 + [shape(2 * D)] * 2,
        scratch_shapes=[
            pltpu.VMEM((PAIRS, 128, 256), BF16), pltpu.VMEM((PAIRS, 128, 256), BF16),
            pltpu.VMEM((256, 256), BF16), pltpu.VMEM((ROWS, 4 * D), F32),
        ],
        compiler_params=params("arbitrary"),
        cost_estimate=cost(2 * count * D * 3 * D, 14 * count * D + 6 * D * D, 4 * count * D),
    )(lengths, tokens, w, bias, gain, shift, fmap)


def value_pair(v_pair):
    low = lanes(v_pair.shape) < HD
    wide = v_pair.astype(F32)
    return (
        jnp.where(low, wide, 1.0).astype(BF16),
        jnp.where(low, swap_halves(wide), 1.0).astype(BF16),
    )


def attend_kernel(len_ref, pq_ref, pk_ref, v_ref, o_ref, rd_ref, s_ref, state):
    step = pl.program_id(0)

    @pl.when(step == 0)
    def _():
        state[...] = jnp.zeros_like(state)

    row = lax.broadcasted_iota(jnp.int32, (CHUNK, CHUNK), 0)
    col = lax.broadcasted_iota(jnp.int32, (CHUNK, CHUNK), 1)
    causal = row >= col
    low = col < HD
    live = (step * CHUNK + row < len_ref[0]).astype(F32)
    for pair in range(PAIRS):
        values = value_pair(v_ref[:, pair * 128 : (pair + 1) * 128])
        sums = []
        for half in range(2):
            head = 2 * pair + half
            cols = slice(head * 128, (head + 1) * 128)
            pq, pk, vx = pq_ref[:, cols], pk_ref[:, cols], values[half]
            prior = state[head].astype(BF16)
            s_ref[0, head] = prior
            scores = jnp.where(causal, nt(pq, pk), 0.0).astype(BF16)
            sums.append(
                nn(jnp.concatenate([scores, pq], 1), jnp.concatenate([vx, prior], 0))
            )
            state[head] += tn(pk, vx)
        numer = jnp.where(low, sums[0], swap_halves(sums[1]))
        denom = jnp.where(low, swap_halves(sums[0]), sums[1])
        rd = live / denom
        rd_ref[:, pair * 128 : (pair + 1) * 128] = rd
        o_ref[:, pair * 128 : (pair + 1) * 128] = (numer * rd).astype(BF16)


def attend(lengths, pq, pk, v):
    count = v.shape[0]
    steps = count // CHUNK
    return pl.pallas_call(
        attend_kernel,
        name="attend",
        grid=(steps,),
        in_specs=[SMEM, rows_of(CHUNK, 2 * D), rows_of(CHUNK, 2 * D), rows_of(CHUNK, D)],
        out_specs=[
            rows_of(CHUNK, D), rows_of(CHUNK, D), pl.BlockSpec((1, HEADS, 128, 128), lambda i: (i, 0, 0, 0)),
        ],
        out_shape=[
            jax.ShapeDtypeStruct((count, D), BF16),
            jax.ShapeDtypeStruct((count, D), F32),
            jax.ShapeDtypeStruct((steps, HEADS, 128, 128), BF16),
        ],
        scratch_shapes=[pltpu.VMEM((HEADS, 128, 128), F32)],
        compiler_params=params("arbitrary"),
        cost_estimate=cost(2 * count * HEADS * 128 * 512, 20 * count * D),
    )(lengths, pq, pk, v)


CUBE = 0.044715
ROOT = 0.7978845608028654


def widen_kernel(
    o_ref, tok_ref, wo_ref, bo_ref, gain_ref, shift_ref, wf_ref, bf_ref, x1_ref, h2_ref, g_ref, slope_ref
):
    x1 = tok_ref[...].astype(F32) + (nn(o_ref[...], wo_ref[...]) + bo_ref[...])
    x1_ref[...] = x1
    unit, _ = normalized(x1)
    h2 = (unit * gain_ref[...] + shift_ref[...]).astype(BF16)
    h2_ref[...] = h2
    for part in range(4):
        cols = slice(part * D, (part + 1) * D)
        f = nn(h2, wf_ref[:, cols]) + bf_ref[:, cols]
        square = f * f
        bend = jnp.tanh(f * (ROOT + (ROOT * CUBE) * square))
        half = 0.5 * f
        g_ref[:, cols] = (half + half * bend).astype(BF16)
        slope = (0.5 + 0.5 * bend) + half * (1.0 - bend * bend) * (ROOT + (3.0 * ROOT * CUBE) * square)
        slope_ref[:, cols] = slope.astype(BF16)


def widen(o, tokens, wo, bo, gain, shift, wf, bf):
    count = tokens.shape[0]
    return pl.pallas_call(
        widen_kernel,
        name="widen",
        grid=(count // ROWS,),
        in_specs=[
            rows_of(ROWS, D), rows_of(ROWS, D), whole((D, D)), whole((1, D)), whole((1, D)), whole((1, D)),
            whole((D, FF)), whole((1, FF)),
        ],
        out_specs=[rows_of(ROWS, D), rows_of(ROWS, D), rows_of(ROWS, FF), rows_of(ROWS, FF)],
        out_shape=[
            jax.ShapeDtypeStruct((count, D), F32), jax.ShapeDtypeStruct((count, D), BF16),
            jax.ShapeDtypeStruct((count, FF), BF16), jax.ShapeDtypeStruct((count, FF), BF16),
        ],
        compiler_params=params("arbitrary"),
        cost_estimate=cost(2 * count * D * 5 * D, 26 * count * D + 10 * D * D, count * FF),
    )(o, tokens, wo, bo, gain, shift, wf, bf)


def add_columns(step, out, values):
    total = jnp.sum(values, 0, keepdims=True)

    @pl.when(step == 0)
    def _():
        out[...] = total

    @pl.when(step > 0)
    def _():
        out[...] += total


def ffn_back_kernel(
    cot_ref, slope_ref, x1_ref, wp_ref, wf_ref, wo_ref, gain_ref,
    df_ref, dx1_ref, da_ref, do_ref, projb_ref, fcb_ref, gain2_ref, bias2_ref, outb_ref,
):
    step = pl.program_id(0)
    cot = cot_ref[...]
    total = jnp.zeros((ROWS, D), F32)
    for part in range(4):
        cols = slice(part * D, (part + 1) * D)
        df = (nt(cot, wp_ref[cols, :]) * slope_ref[:, cols].astype(F32)).astype(BF16)
        df_ref[:, cols] = df
        add_columns(step, fcb_ref.at[:, cols], df.astype(F32))
        total = total + nt(df, wf_ref[:, cols])
    unit, scale = normalized(x1_ref[...])
    wide = cot.astype(F32)
    dx1 = wide + norm_back(total, gain_ref[...], unit, scale)
    dx1_ref[...] = dx1
    da = dx1.astype(BF16)
    da_ref[...] = da
    do_ref[...] = nt(da, wo_ref[...]).astype(BF16)
    add_columns(step, projb_ref, wide)
    add_columns(step, gain2_ref, total * unit)
    add_columns(step, bias2_ref, total)
    add_columns(step, outb_ref, da.astype(F32))


def ffn_back(cot, slope, x1, wp, wf, wo, gain):
    count = cot.shape[0]
    rows = lambda width, kind=BF16: jax.ShapeDtypeStruct((count, width), kind)
    column = lambda width: jax.ShapeDtypeStruct((1, width), F32)
    return pl.pallas_call(
        ffn_back_kernel,
        name="ffn_back",
        grid=(count // ROWS,),
        in_specs=[
            rows_of(ROWS, D), rows_of(ROWS, FF), rows_of(ROWS, D), whole((FF, D)), whole((D, FF)), whole((D, D)), whole((1, D)),
        ],
        out_specs=[rows_of(ROWS, FF), rows_of(ROWS, D), rows_of(ROWS, D), rows_of(ROWS, D)]
        + [whole((1, D), False), whole((1, FF), False)]
        + [whole((1, D), False)] * 3,
        out_shape=[rows(FF), rows(D, F32), rows(D), rows(D), column(D), column(FF), column(D), column(D), column(D)],
        compiler_params=params("arbitrary"),
        cost_estimate=cost(2 * count * D * 9 * D, 30 * count * D + 18 * D * D),
    )(cot, slope, x1, wp, wf, wo, gain)


def attend_back_kernel(
    do_ref, rd_ref, o_ref, pq_ref, pk_ref, v_ref, s_ref, q_ref, k_ref, map_ref,
    dproj_ref, sums_ref, fmap_ref, fq, fk, ones, state, gq, gk,
):
    step = pl.program_id(0)

    @pl.when(step == 0)
    def _():
        build_maps(map_ref, fq, fk)
        ones[...] = block_ones(4 * HD)
        state[...] = jnp.zeros_like(state)
        gq[...] = jnp.zeros_like(gq)
        gk[...] = jnp.zeros_like(gk)

    row = lax.broadcasted_iota(jnp.int32, (CHUNK, CHUNK), 0)
    col = lax.broadcasted_iota(jnp.int32, (CHUNK, CHUNK), 1)
    causal = row >= col
    below = row <= col
    low = col < HD
    for pair in range(PAIRS):
        cols = slice(pair * 128, (pair + 1) * 128)
        numer_grad = (do_ref[:, cols].astype(F32) * rd_ref[:, cols]).astype(BF16).astype(F32)
        product = numer_grad * o_ref[:, cols].astype(F32)
        coarse = product.astype(BF16)
        fine = (product - coarse.astype(F32)).astype(BF16)
        dot_ones = ones[0:128, 0:128]
        denom_grad = -nn(jnp.concatenate([coarse, fine], 1), jnp.concatenate([dot_ones, dot_ones], 0))
        turned_grad = swap_halves(numer_grad)
        values = value_pair(v_ref[:, cols])
        grads = []
        for numer, denom in ((numer_grad, swap_halves(denom_grad)), (turned_grad, denom_grad)):
            rounded = denom.astype(BF16).astype(F32)
            tail = jnp.where(col == HD, rounded, jnp.where(col == HD + 1, denom - rounded, 0.0))
            grads.append(jnp.where(low, numer, tail).astype(BF16))
        query_grads, key_grads, value_grads = [], [], []
        for half in range(2):
            head = 2 * pair + half
            wide = slice(head * 128, (head + 1) * 128)
            pq, pk, vx, dn = pq_ref[:, wide], pk_ref[:, wide], values[half], grads[half]
            later = state[head].astype(BF16)
            scores_t = jnp.where(below, nt(pk, pq), 0.0).astype(BF16)
            dscores = jnp.where(causal, nt(dn, vx), 0.0).astype(BF16)
            dscores_t = jnp.where(below, nt(vx, dn), 0.0).astype(BF16)
            query_grads.append(nn(dscores, pk) + nt(dn, s_ref[0, head]))
            key_grads.append(nn(dscores_t, pq) + nt(vx, later))
            value_grads.append(nn(jnp.concatenate([scores_t, pk], 1), jnp.concatenate([dn, later], 0)))
            state[head] += tn(pq, dn)
        dv = jnp.where(low, value_grads[0], swap_halves(value_grads[1])).astype(BF16)
        dproj_ref[:, 2 * D + pair * 128 : 2 * D + (pair + 1) * 128] = dv
        both = slice(pair * 256, (pair + 1) * 256)
        for part, (grad, feat_ref, rows_ref, maps, total) in enumerate(
            ((query_grads, pq_ref, q_ref, fq, gq), (key_grads, pk_ref, k_ref, fk, gk))
        ):
            grad = jnp.concatenate(grad, 1)
            feat = feat_ref[:, both].astype(F32)
            inner = nn((grad * feat).astype(BF16), ones[...])
            logit = (feat * (grad - inner)).astype(BF16)
            dproj_ref[:, part * D + pair * 128 : part * D + (pair + 1) * 128] = nt(logit, maps[pair]).astype(BF16)
            total[pair] += tn(rows_ref[:, cols], logit)
    add_columns(step, sums_ref, dproj_ref[...].astype(F32))

    @pl.when(step == pl.num_programs(0) - 1)
    def _():
        first = lanes((HD, 2 * HD)) < HD
        for head in range(HEADS):
            r, c = (head % 2) * HD, (head % 2) * 2 * HD
            bq = gq[head // 2, r : r + HD, c : c + 2 * HD]
            bk = gk[head // 2, r : r + HD, c : c + 2 * HD]
            fmap_ref[head * HD : (head + 1) * HD, :] = jnp.where(first, bq - swap_halves(bq), swap_halves(bk) - bk)


def attend_back(do, rd, o, pq, pk, v, s, q, k, fmap):
    count = v.shape[0]
    steps = count // CHUNK
    back = lambda width: pl.BlockSpec((CHUNK, width), lambda i: (steps - 1 - i, 0))
    return pl.pallas_call(
        attend_back_kernel,
        name="attend_back",
        grid=(steps,),
        in_specs=[
            back(D), back(D), back(D), back(2 * D), back(2 * D), back(D),
            pl.BlockSpec((1, HEADS, 128, 128), lambda i: (steps - 1 - i, 0, 0, 0)),
            back(D), back(D), whole((D, 2 * HD)),
        ],
        out_specs=[back(3 * D), whole((1, 3 * D), False), whole((D, 2 * HD), False)],
        out_shape=[
            jax.ShapeDtypeStruct((count, 3 * D), BF16), jax.ShapeDtypeStruct((1, 3 * D), F32),
            jax.ShapeDtypeStruct((D, 2 * HD), F32),
        ],
        scratch_shapes=[
            pltpu.VMEM((PAIRS, 128, 256), BF16), pltpu.VMEM((PAIRS, 128, 256), BF16), pltpu.VMEM((256, 256), BF16),
            pltpu.VMEM((HEADS, 128, 128), F32), pltpu.VMEM((PAIRS, 128, 256), F32), pltpu.VMEM((PAIRS, 128, 256), F32),
        ],
        compiler_params=params("arbitrary"),
        cost_estimate=cost(2 * count * HEADS * 128 * 128 * 14, 40 * count * D),
    )(do, rd, o, pq, pk, v, s, q, k, fmap)


def outer_kernel(left_ref, right_ref, out_ref):
    out_ref[...] = tn(left_ref[...], right_ref[...]).astype(BF16)


def outer(left, right, tile=256):
    count, wide = left.shape
    across = right.shape[1]
    return pl.pallas_call(
        outer_kernel,
        name="outer",
        grid=(wide // tile,),
        in_specs=[pl.BlockSpec((count, tile), lambda i: (0, i)), whole((count, across))],
        out_specs=pl.BlockSpec((tile, across), lambda i: (i, 0)),
        out_shape=jax.ShapeDtypeStruct((wide, across), BF16),
        compiler_params=params("arbitrary"),
        cost_estimate=cost(2 * count * wide * across, 2 * (count * (wide + across) + wide * across)),
    )(left, right)


def input_back_kernel(dproj_ref, w_ref, tok_ref, dx1_ref, gain_ref, out_ref, gain1_ref, bias1_ref):
    step = pl.program_id(0)
    grad = nt(dproj_ref[...], w_ref[...])
    unit, scale = normalized(tok_ref[...].astype(F32))
    out_ref[...] = (dx1_ref[...] + norm_back(grad, gain_ref[...], unit, scale)).astype(BF16)
    add_columns(step, gain1_ref, grad * unit)
    add_columns(step, bias1_ref, grad)


def input_back(dproj, w, tokens, dx1, gain):
    count = tokens.shape[0]
    column = jax.ShapeDtypeStruct((1, D), F32)
    return pl.pallas_call(
        input_back_kernel,
        name="input_back",
        grid=(count // ROWS,),
        in_specs=[rows_of(ROWS, 3 * D), whole((D, 3 * D)), rows_of(ROWS, D), rows_of(ROWS, D), whole((1, D))],
        out_specs=[rows_of(ROWS, D), whole((1, D), False), whole((1, D), False)],
        out_shape=[jax.ShapeDtypeStruct((count, D), BF16), column, column],
        compiler_params=params("arbitrary"),
        cost_estimate=cost(2 * count * D * 3 * D, 14 * count * D + 6 * D * D),
    )(dproj, w, tokens, dx1, gain)


def narrow_kernel(g_ref, w_ref, bias_ref, x1_ref, out_ref):
    out_ref[...] = (x1_ref[...] + (nn(g_ref[...], w_ref[...]) + bias_ref[...])).astype(BF16)


def narrow(g, w, bias, x1):
    count = g.shape[0]
    return pl.pallas_call(
        narrow_kernel,
        name="narrow",
        grid=(count // ROWS,),
        in_specs=[rows_of(ROWS, FF), whole((FF, D)), whole((1, D)), rows_of(ROWS, D)],
        out_specs=rows_of(ROWS, D),
        out_shape=jax.ShapeDtypeStruct((count, D), BF16),
        compiler_params=params("arbitrary"),
        cost_estimate=cost(2 * count * D * FF, 14 * count * D + 8 * D * D),
    )(g, w, bias, x1)


def on_device(
    tokens, lengths, qkv_weight, qkv_bias, out_weight, out_bias, fc_weight, fc_bias, proj_weight, proj_bias,
    norm1_gain, norm1_bias, norm2_gain, norm2_bias, feature_map, cotangent,
):
    gather = lambda value: lax.all_gather(value, "fsdp", axis=0, tiled=True)
    w_qkv, w_out, w_fc, w_proj, fmap = map(gather, (qkv_weight, out_weight, fc_weight, proj_weight, feature_map))
    small = [qkv_bias, out_bias, fc_bias, proj_bias, norm1_gain, norm1_bias, norm2_gain, norm2_bias]
    packed = gather(jnp.concatenate(small)[None])
    bounds = [0]
    for value in small:
        bounds.append(bounds[-1] + value.shape[0])
    b_qkv, b_out, b_fc, b_proj, g1, s1, g2, s2 = (
        packed[:, a:b].reshape(1, -1).astype(F32) for a, b in zip(bounds[:-1], bounds[1:])
    )
    h1, q, k, v, pq, pk = project(lengths, tokens, w_qkv, b_qkv, g1, s1, fmap)
    o, rd, s = attend(lengths, pq, pk, v)
    x1, h2, g, slope = widen(o, tokens, w_out, b_out, g2, s2, w_fc, b_fc)
    projw_grad = outer(g, cotangent)
    df, dx1, da, do, projb, fcb, gain2, bias2, outb = ffn_back(cotangent, slope, x1, w_proj, w_fc, w_out, g2)
    fcw_grad = outer(h2, df)
    outw_grad = outer(o, da)
    dproj, sums, fmap_grad = attend_back(do, rd, o, pq, pk, v, s, q, k, fmap)
    qkvw_grad = outer(h1, dproj)
    input_grad, gain1, bias1 = input_back(dproj, w_qkv, tokens, dx1, g1)
    block_out = narrow(g, w_proj, b_proj, x1)

    def owned(value):
        share = lax.psum_scatter(value.astype(BF16), "fsdp", scatter_dimension=0, tiled=True)
        return lax.psum(share, "dp").astype(F32)

    shards = lax.axis_size("fsdp")
    vectors = [sums[0, : 2 * D], sums[0, 2 * D :], outb[0], fcb[0], projb[0], gain1[0], bias1[0], gain2[0], bias2[0]]
    packed = jnp.concatenate([vector.reshape(shards, -1) for vector in vectors], 1)
    mine = owned(packed)[0]
    bounds = [0]
    for vector in vectors:
        bounds.append(bounds[-1] + vector.shape[0] // shards)
    qkb, vb, outb, fcb, projb, gain1, bias1, gain2, bias2 = (mine[a:b] for a, b in zip(bounds[:-1], bounds[1:]))
    return (
        block_out, input_grad, owned(qkvw_grad), qkb, vb, owned(outw_grad), outb, owned(fcw_grad), fcb,
        owned(projw_grad), projb, gain1, bias1, gain2, bias2, owned(fmap_grad),
    )


def solution(mesh):
    rows = P(("dp", "fsdp"), None)
    wide = P("fsdp", None)
    flat = P("fsdp")
    in_specs = (
        rows, P(("dp", "fsdp")), wide, flat, wide, flat, wide, flat, wide, flat, flat, flat, flat, flat, wide, rows,
    )
    out_specs = (rows, rows, wide, flat, flat, wide, flat, wide, flat, wide, flat, flat, flat, flat, flat, wide)
    return jax.shard_map(on_device, mesh=mesh, in_specs=in_specs, out_specs=out_specs, check_vma=False)
```

time: 798 us -> 542 us (0.68)
  matrix products: 194 us -> 0 us
  Pallas kernels: 0 us -> 189 us
  local copies, waits for them, and re-layouts: 180 us -> 16.7 us
  other arithmetic: 94.8 us -> 9.2 us
  waiting for transfers between devices: 216 us -> 230 us
    pallas_call x0 -> x11, Pallas kernels: none -> 189 us  [the longest x1 52.1 us: attend_back(): pl.pallas_call(attend_back_kernel, name='attend_back', grid=(steps,), in_...]
    dot_general x30 -> x0, matrix products: 176 us -> none  [the longest x4 39.1 us: back_dot(): lax.dot_general(left, right, (((1,), (1,)), ((), ())), preferred_element_...]
    unnamed x255 -> x21, local copies, waits for them, and re-layouts: 46.3 us -> 3.84 us
    concatenate x10 -> x2, local copies, waits for them, and re-layouts: 47.2 us -> 5.56 us  [the longest x1 5.47 us: on_device(): packed = gather(jnp.concatenate(small)[None])]
    all_gather x4, waiting for transfers between devices: 0.01 us -> 40.7 us  [on_device(): gather = lambda value: lax.all_gather(value, 'fsdp', axis=0, tiled=True)]
    reduce_sum x15 -> x0, other arithmetic: 36.9 us -> none  [the longest x3 8.4 us: norm_rows(): return centred * lax.rsqrt(spread + EPSILON) * scale_row + shift_row]
    convert_element_type x32 -> x9, other arithmetic: 32 us -> 8.36 us  [the longest x6 7.58 us: owned(): return lax.psum(share, 'dp').astype(F32)]
    reduce_scatter x5, waiting for transfers between devices: 158 us -> 138 us  [owned(): lax.psum_scatter(value.astype(BF16), 'fsdp', scatter_dimension=0, tiled=T...]
  transfers between devices with their start and end apart: 10 -> 10, of which waited for: 5 -> 6; matrix products, arithmetic and copies ran while one was open for 47% -> 3% of each run, Pallas kernels for 0% -> 29%
where the time goes in v1:
time: 542 us; the launch traced here: 541 us
  waiting for transfers between devices  230 us (42%)
  Pallas kernels  189 us (35%)
  blocking collectives  80.4 us (15%)
  local copies, waits for them, and re-layouts  16.7 us (3%)
  between operations  15.6 us (3%)
  other arithmetic  9.2 us (2%)
    reduce_scatter x5, waiting for transfers between devices, owned(): lax.psum_scatter(value.astype(BF16), 'fsdp', scatter_dimension=0, tiled=T...  138 us
    pallas_call x1, Pallas kernels, attend_back(): pl.pallas_call(attend_back_kernel, name='attend_back', grid=(steps,), in_...  52.1 us
    unnamed x2, blocking collectives  49.2 us
    psum x1, waiting for transfers between devices, owned(): return lax.psum(share, 'dp').astype(F32)  49 us
    all_gather x4, waiting for transfers between devices, on_device(): gather = lambda value: lax.all_gather(value, 'fsdp', axis=0, tiled=True)  40.7 us
    pallas_call x4, Pallas kernels, outer(): pl.pallas_call(outer_kernel, name='outer', grid=(wide // tile,), in_specs...  35.5 us
    pallas_call x1, Pallas kernels, ffn_back(): pl.pallas_call(ffn_back_kernel, name='ffn_back', grid=(count // ROWS,), i...  27 us
    psum x1, blocking collectives, owned(): return lax.psum(share, 'dp').astype(F32)  21.2 us
  transfers between devices with their start and end apart: 10, of which 6 were waited for; matrix products, arithmetic and copies ran while one was open for 3% of the time, Pallas kernels for 29%

profile of v1, /device:TPU:0, one launch (start us, length us, event | category | flops | bytes accessed | tf_op | source)
XLA Modules:
  0.0 541.1 jit_solution(6163685168147431733)
XLA Ops:
  7.2 0.7 all-gather.6.cloned.1.call-update
  8.0 0.7 all-gather.8.cloned.1.call-update
  8.7 0.7 all-gather.10.cloned.1.call-update
  9.4 0.5 all-gather.12.cloned.1.call-update
  10.7 1.3 fusion
  12.6 5.5 %concatenate.7 = bf16[1248]{0:T(1024)(128)(2,1)S(1)} concatenate(bf16[288]{0:T(512)(128)(2,1)} %param.19, bf16[96]{0:T(256)(128)(2,1)} %param.21, bf16[384]{0:T(512)(128)(2,1)} %param.23, bf16[96]{0:T(256)(128)(2,1)} %param.25, bf16[96]{0:T(256)(128)(2,1)} %param.26, bf16[96]{0:T(256)(128)(2,1)} %param.27, bf16[96]{0:T(256)(128)(2,1)} %param.28, bf16[96]{0:T(256)(128)(2,1)} %param.29), dimensions={0} | concatenate | bytes 4992 | tf_op jit(solution)/shard_map/concatenate | solution.py:501
  18.1 0.3 dynamic-update-slice
  18.4 26.1 %all-reduce = bf16[9984]{0:T(1024)(128)(2,1)S(1)} all-reduce(bf16[9984]{0:T(1024)(128)(2,1)S(1)} %dynamic-update-slice), channel_id=2, replica_groups=mesh['dp'=4,'fsdp'=8] {'fsdp'}, use_global_device_ids=true, to_apply=%add | all-reduce | flops 9984 | bytes 39936
  44.6 0.6 copy.32
  45.2 0.7 reshape.161.bias_ref
  46.0 0.7 reshape.165.gain_ref
  46.7 0.7 reshape.162.gain_ref
  47.3 0.7 reshape.166.shift_ref
  48.0 0.7 reshape.164.bo_ref
  48.6 0.7 reshape.163.shift_ref
  49.3 10.0 %all_gather.20.map_ref = bf16[768,128]{1,0:T(8,128)(2,1)} all-gather(bf16[96,128]{1,0:T(8,128)(2,1)} %param.30), channel_id=1, replica_groups=mesh['dp'=4,'fsdp'=8] {'fsdp'}, dimensions={0}, use_global_device_ids=true | all-gather | bytes 221184 | tf_op jit(solution)/shard_map/all_gather | solution.py:498
  59.3 15.7 %project.1 = (bf16[1024,768]{1,0:T(8,128)(2,1)}, bf16[1024,768]{1,0:T(8,128)(2,1)}, bf16[1024,768]{1,0:T(8,128)(2,1)}, bf16[1024,768]{1,0:T(8,128)(2,1)}, bf16[1...) custom-call(s32[1]{0:T(128)S(6)} %copy.38.len_ref, bf16[1024,768]{1,0:T(8,128)(2,1)} %tok_ref.5, ...), custom_call_target="tpu_custom_call" | custom-call | flops 3623878656 | bytes 14548992 | tf_op jit(solution)/shard_map/project/pallas_call | solution.py:152
  75.0 18.7 %attend.1 = (bf16[1024,768]{1,0:T(8,128)(2,1)}, f32[1024,768]{1,0:T(8,128)}, bf16[8,12,128,128]{3,2,1,0:T(8,128)(2,1)}) custom-call(s32[1]{0:T(128)S(6)} %copy.38.len_ref, bf16[1024,1536]{1,0:T(8,128)(2,1)} %get-tuple-element.44.pq_ref, bf16[1024,1536]{1,0:T(8,128)(2,1)} %get-tuple-element.45.pk_ref, bf16[1024,768]{1,0:T(8,128)(2,1)} %get-tuple-element.46.v_ref), custom_call_target="tpu_custom_call" | custom-call | flops 1610612736 | bytes 15728640 | tf_op jit(solution)/shard_map/attend/pallas_call | solution.py:215
  93.7 20.1 %all-gather.10.cloned.1.call-done.wf_ref = bf16[768,3072]{1,0:T(8,128)(2,1)} async-done(((bf16[96,3072]{1,0:T(8,128)(2,1)}), bf16[768,3072]{1,0:T(8,128)(2,1)}) %all-gather.10.cloned.1.call-update) | async-done | bytes 4718608 | tf_op jit(solution)/shard_map/all_gather | solution.py:498
  113.7 20.1 %widen.1 = (f32[1024,768]{1,0:T(8,128)}, bf16[1024,768]{1,0:T(8,128)(2,1)}, bf16[1024,3072]{1,0:T(8,128)(2,1)}, bf16[1024,3072]{1,0:T(8,128)(2,1)}) custom-call(bf16[1024,768]{1,0:T(8,128)(2,1)} %get-tuple-element.47.o_ref.left_ref, bf16[1024,768]{1,0:T(8,128)(2,1)} %tok_ref.5, bf16[768,768]{1,0:T(8,128)(2,1)} %all-gather.8.cloned.1.call-done.wo_ref, ...), custom_call_target="tpu_custom_call" | custom-call | flops 6039797760 | bytes 26345472 | tf_op jit(solution)/shard_map/widen/pallas_call | solution.py:259
  133.8 20.6 %all-gather.12.cloned.1.call-done.w_ref.wp_ref = bf16[3072,768]{1,0:T(8,128)(2,1)} async-done(((bf16[384,768]{1,0:T(8,128)(2,1)}), bf16[3072,768]{1,0:T(8,128)(2,1)}) %all-gather.12.cloned.1.call-update) | async-done | bytes 4718608 | tf_op jit(solution)/shard_map/all_gather | solution.py:498
  154.4 27.0 %ffn_back.1 = (bf16[1024,3072]{1,0:T(8,128)(2,1)}, f32[1024,768]{1,0:T(8,128)}, bf16[1024,768]{1,0:T(8,128)(2,1)}, bf16[1024,768]{1,0:T(8,128)(2,1)}, f32[1,768]...) custom-call(bf16[1024,768]{1,0:T(8,128)(2,1)} %right_ref.1, ...), custom_call_target="tpu_custom_call" | custom-call | flops 10871635968 | bytes 34209792 | tf_op jit(solution)/shard_map/ffn_back/pallas_call | solution.py:319
  181.4 4.8 outer.5
  186.3 52.1 %attend_back.1 = (bf16[1024,2304]{1,0:T(8,128)(2,1)}, f32[1,2304]{1,0:T(1,128)}, f32[768,128]{1,0:T(8,128)}) custom-call(bf16[1024,768]{1,0:T(8,128)(2,1)} %get-tuple-element.51.do_ref, f32[1024,768]{1,0:T(8,128)} %get-tuple-element.52.rd_ref, bf16[1024,768]{1,0:T(8,128)(2,1)} %get-tuple-element.47.o_ref.left_ref, ...), custom_call_target="tpu_custom_call" | custom-call | flops 5637144576 | bytes 31457280 | tf_op jit(solution)/shard_map/attend_back/pallas_call | solution.py:410
  238.4 7.9 %outer.4 = bf16[768,2304]{1,0:T(8,128)(2,1)} custom-call(bf16[1024,768]{1,0:T(8,128)(2,1)} %get-tuple-element.59.left_ref, bf16[1024,2304]{1,0:T(8,128)(2,1)} %get-tuple-element.56.dproj_ref.right_ref), custom_call_target="tpu_custom_call" | custom-call | flops 3623878656 | bytes 9830400 | tf_op jit(solution)/shard_map/outer/pallas_call | solution.py:440
  246.3 13.1 %outer.7 = bf16[3072,768]{1,0:T(8,128)(2,1)} custom-call(bf16[1024,3072]{1,0:T(8,128)(2,1)} %get-tuple-element.48.g_ref.left_ref, bf16[1024,768]{1,0:T(8,128)(2,1)} %right_ref.1), custom_call_target="tpu_custom_call" | custom-call | flops 4831838208 | bytes 12582912 | tf_op jit(solution)/shard_map/outer/pallas_call | solution.py:440
  259.5 9.8 %outer.6 = bf16[768,3072]{1,0:T(8,128)(2,1)} custom-call(bf16[1024,768]{1,0:T(8,128)(2,1)} %get-tuple-element.69.left_ref, bf16[1024,3072]{1,0:T(8,128)(2,1)} %get-tuple-element.70.right_ref), custom_call_target="tpu_custom_call" | custom-call | flops 4831838208 | bytes 12582912 | tf_op jit(solution)/shard_map/outer/pallas_call | solution.py:440
  269.3 0.9 copy-done.1
  270.2 0.7 convert_element_type.83
  271.2 0.7 reshape.168.bias_ref
  272.1 22.4 %reduce-scatter.6.cloned.1.call-done = bf16[96,2304]{1,0:T(8,128)(2,1)} async-done(((bf16[768,2304]{1,0:T(8,128)(2,1)}), bf16[96,2304]{1,0:T(8,128)(2,1)}) %reduce-scatter.6.cloned.1.call-update) | async-done | bytes 442384 | tf_op jit(solution)/shard_map/reduce_scatter | solution.py:521
  294.6 57.8 %reduce-scatter.12.cloned.1.call-done = bf16[384,768]{1,0:T(8,128)(2,1)} async-done(((bf16[3072,768]{1,0:T(8,128)(2,1)}), bf16[384,768]{1,0:T(8,128)(2,1)}) %reduce-scatter.12.cloned.1.call-update) | async-done | bytes 589840 | tf_op jit(solution)/shard_map/reduce_scatter | solution.py:521
  352.3 57.4 %reduce-scatter.10.cloned.1.call-done = bf16[96,3072]{1,0:T(8,128)(2,1)} async-done(((bf16[768,3072]{1,0:T(8,128)(2,1)}), bf16[96,3072]{1,0:T(8,128)(2,1)}) %reduce-scatter.10.cloned.1.call-update) | async-done | bytes 589840 | tf_op jit(solution)/shard_map/reduce_scatter | solution.py:521
  409.8 9.8 %input_back.1 = (bf16[1024,768]{1,0:T(8,128)(2,1)}, f32[1,768]{1,0:T(1,128)}, f32[1,768]{1,0:T(1,128)}) custom-call(bf16[1024,2304]{1,0:T(8,128)(2,1)} %get-tuple-element.56.dproj_ref.right_ref, bf16[768,2304]{1,0:T(8,128)(2,1)} %all-gather.6.cloned.1.call-done.w_ref, bf16[1024,768]{1,0:T(8,128)(2,1)} %tok_ref.5, f32[1024,768]{1,0:T(8,128)} %get-tuple-element.57.dx1_ref, ...), custom_call_target="tpu_custom_call" | custom-call | flops 3623878656 | bytes 14548992 | tf_op jit(solution)/shard_map/input_back/pallas_call | solution.py:464
  419.6 0.7 convert_reduce_fusion.3
  421.1 23.1 %all-reduce.1 = bf16[8,1248]{1,0:T(8,128)(2,1)S(1)} all-reduce(bf16[8,1248]{1,0:T(8,128)(2,1)S(1)} %concatenate.8), channel_id=4, replica_groups=mesh['dp'=4,'fsdp'=8] {'fsdp'}, use_global_device_ids=true, to_apply=%region_2.0.clone | all-reduce | flops 9984 | bytes 39936
  444.1 0.7 constant_dynamic-slice_fusion
  444.8 9.9 %narrow.1 = bf16[1024,768]{1,0:T(8,128)(2,1)} custom-call(bf16[1024,3072]{1,0:T(8,128)(2,1)} %get-tuple-element.48.g_ref.left_ref, bf16[3072,768]{1,0:T(8,128)(2,1)} %all-gather.12.cloned.1.call-done.w_ref.wp_ref, f32[1,768]{1,0:T(1,128)} %reshape.168.bias_ref, f32[1024,768]{1,0:T(8,128)} %get-tuple-element.49.x1_ref), custom_call_target="tpu_custom_call" | custom-call | flops 4831838208 | bytes 15728640 | tf_op jit(solution)/shard_map/narrow/pallas_call | solution.py:482
  454.7 21.2 %all-reduce.2 = (bf16[1,1248]{1,0:T(2,128)(2,1)S(1)}, bf16[96,128]{1,0:T(8,128)(2,1)S(1)}) all-reduce(bf16[1,1248]{1,0:T(2,128)(2,1)S(1)} %constant_dynamic-slice_fusion, bf16[96,128]{1,0:T(8,128)(2,1)} %reduce-scatter.14.cloned.1.call-done), channel_id=1, replica_groups=mesh['dp'=4,'fsdp'=8] {'dp'}, use_global_device_ids=true, to_apply=%region_3.0 | all-reduce | flops 13536 | bytes 54144 | tf_op jit(solution)/shard_map/psum | solution.py:522
  475.9 0.6 slice.124
  476.5 0.6 convert_element_type.84
  477.1 0.6 slice_reduce_fusion.2
  477.7 0.6 slice_bitcast_fusion
  478.3 49.0 %all-reduce.6.cloned.1.call-done = (bf16[96,2304]{1,0:T(8,128)(2,1)}, bf16[96,768]{1,0:T(8,128)(2,1)}, bf16[96,3072]{1,0:T(8,128)(2,1)}, bf16[384,768]{1,0:T(8,128)(2,1)}) async-done(((bf16[96,2304]{1,0:T(8,128)(2,1)}, bf16[96,768]{1,0:T(8,128)(2,1)}, bf16[96,3072]{1,0:T(8,128)(2,1)}, bf16[384,768]{1,0:T(8,128)(2,1)}), (bf16[96,2304]{1,0:T(8,128)(2,1)}, bf16[96,768]{1,0:T(8,128)(2,1)}, ...) | async-done | bytes 1769488 | tf_op jit(solution)/shard_map/psum | solution.py:522
  527.3 1.7 convert_element_type.80
  529.0 2.0 convert_element_type.78
  531.0 2.2 convert_element_type.81
  533.2 1.1 convert_element_type.82
  (57 shorter events, 1.9 us)
Async XLA Ops:
  7.2 52.1 %all-gather.6.cloned.1.call-start = ((), (), s32[]{:S(2)}) async-start(), calls=%async_computation.5 | async-start | bytes 3981312 | tf_op jit(solution)/shard_map/all_gather | solution.py:498
  7.9 85.8 %all-gather.8.cloned.1.call-start = ((), (), s32[]{:S(2)}) async-start(), calls=%async_computation.6 | async-start | bytes 1327104 | tf_op jit(solution)/shard_map/all_gather | solution.py:498
  8.7 105.1 %all-gather.10.cloned.1.call-start = ((), (), s32[]{:S(2)}) async-start(), calls=%async_computation.7 | async-start | bytes 5308416 | tf_op jit(solution)/shard_map/all_gather | solution.py:498
  9.4 145.0 %all-gather.12.cloned.1.call-start = ((), (), s32[]{:S(2)}) async-start(), calls=%async_computation.8 | async-start | bytes 5308416 | tf_op jit(solution)/shard_map/all_gather | solution.py:498
  10.0 262.2 %reduce-scatter.8.cloned.1.call-start = ((), (), s32[]{:S(2)}) async-start(), calls=%async_computation.10 | async-start | bytes 1327104 | tf_op jit(solution)/shard_map/reduce_scatter | solution.py:521
  186.2 108.4 %reduce-scatter.6.cloned.1.call-start = ((), (), s32[]{:S(2)}) async-start(), calls=%async_computation.9 | async-start | bytes 3981312 | tf_op jit(solution)/shard_map/reduce_scatter | solution.py:521
  246.3 106.0 %reduce-scatter.12.cloned.1.call-start = ((), (), s32[]{:S(2)}) async-start(), calls=%async_computation.12 | async-start | bytes 5308416 | tf_op jit(solution)/shard_map/reduce_scatter | solution.py:521
  259.4 150.3 %reduce-scatter.10.cloned.1.call-start = ((), (), s32[]{:S(2)}) async-start(), calls=%async_computation.11 | async-start | bytes 5308416 | tf_op jit(solution)/shard_map/reduce_scatter | solution.py:521
  269.2 1.0 copy-start.1
  269.2 2.6 copy-start.3
  269.3 185.5 %reduce-scatter.14.cloned.1.call-start = ((), (), s32[]{:S(2)}) async-start(), calls=%async_computation.13 | async-start | bytes 221184 | tf_op jit(solution)/shard_map/reduce_scatter | solution.py:521
  271.0 256.4 %all-reduce.6.cloned.1.call-start = ((), (), s32[]{:S(2)}) async-start(), calls=%async_computation.14 | async-start | bytes 3538944 | tf_op jit(solution)/shard_map/psum | solution.py:522
  409.7 10.7 %copy-start.6 = (f32[1,768]{1,0:T(1,128)S(1)}, f32[1,768]{1,0:T(1,128)}, u32[]{:S(2)}) copy-start(f32[1,768]{1,0:T(1,128)} %get-tuple-element.63) | copy-start | bytes 9220
  409.7 10.7 %copy-start.7 = (f32[1,768]{1,0:T(1,128)S(1)}, f32[1,768]{1,0:T(1,128)}, u32[]{:S(2)}) copy-start(f32[1,768]{1,0:T(1,128)} %get-tuple-element.61) | copy-start | bytes 9220
  409.7 10.9 %copy-start.4 = (f32[1,768]{1,0:T(1,128)S(1)}, f32[1,768]{1,0:T(1,128)}, u32[]{:S(2)}) copy-start(f32[1,768]{1,0:T(1,128)} %get-tuple-element.66) | copy-start | bytes 9220
  409.8 10.9 %copy-start.5 = (f32[1,768]{1,0:T(1,128)S(1)}, f32[1,768]{1,0:T(1,128)}, u32[]{:S(2)}) copy-start(f32[1,768]{1,0:T(1,128)} %get-tuple-element.67) | copy-start | bytes 9220
  409.8 11.1 %copy-start.2 = (f32[1,3072]{1,0:T(1,128)S(1)}, f32[1,3072]{1,0:T(1,128)}, u32[]{:S(2)}) copy-start(f32[1,3072]{1,0:T(1,128)} %get-tuple-element.62) | copy-start | bytes 36868
  527.3 5.9 %copy-start = (bf16[384,768]{1,0:T(8,128)(2,1)S(1)}, bf16[384,768]{1,0:T(8,128)(2,1)}, u32[]{:S(2)}) copy-start(bf16[384,768]{1,0:T(8,128)(2,1)} %get-tuple-element.77) | copy-start | bytes 1769476
Sparse Core Ops, SparseCore 0:
  9.9 36.8 all-gather.5
  48.7 24.0 all-gather.7
  74.7 38.9 all-gather.9
  115.5 38.9 all-gather.11
  186.3 36.9 reduce-scatter.7
  246.4 48.1 reduce-scatter.5
  298.4 53.8 reduce-scatter.11
  355.8 53.8 reduce-scatter.9
  413.6 33.4 reduce-scatter.13
  449.6 77.6 all-reduce.5
